TPU v7x, 512 devices: a whole 4x8x8 slice. The times are simulated.
512 devices in a mesh: inst: 2 (over y_hi), blk: 256 (over z, y_lo, x, core).
Axes of the slice: x: 4, y: 8 (y_hi: 2, y_lo: 4; y = y_hi * 4 + y_lo), z: 8, core: 2. Of those that a mesh axis runs over, the one named last changes fastest.
Arguments:
- state: float32 [8, 5, 256, 32, 256], P('inst', None, 'blk'), as said below
- slot_of: int32 [256], replicated, may hold values from 0 to 255, as said below
- conn_block: int32 [256, 2], replicated, may hold values from 0 to 255, as said below
- conn_side: int32 [256, 2], replicated, may hold values from 0 to 1
- conn_shift: int32 [256, 2], replicated, may hold values from 0 to 255
- rows: int32 [256], replicated, may hold values from 16 to 32
Outputs:
- residual: float32 [8, 5, 256, 32, 256], P('inst', None, 'blk')
Inputs may be any that keep to these rules, and one draw needn't show every extreme that they name: slot_of is a permutation of the block numbers. With d(b) = slot_of[b], the index along blk of the device holding block b, d(conn_block[b, f]) - d(b) taken cyclically modulo the number of blk devices lies within -2 to 2; both ends are reached in every draw. `state`: density and pressure are positive.
All inputs are finite; a program needn't handle non-finite values.
Results may differ from a plain program's by a relative error of at most 0.00012.
Values sent between devices are 32-bit elements; how exact they have to be, the bound alone decides.
A program may use at most 64 MiB of HBM per device.

v0:
```python
import math
import jax
import jax.numpy as jnp
from jax import lax
from jax.sharding import PartitionSpec as P

REACH = 2
GAMMA_MINUS = 0.4
DAMPING = 0.05
FREQUENCY = 1.0


def passed_along(value, axis, steps):
    count = lax.axis_size(axis)
    pairs = [(source, (source + steps) % count) for source in range(count)]
    return lax.ppermute(value, axis, pairs)


def spectral_matrix(count):
    position = jnp.arange(count, dtype=jnp.int32)
    offset = position[:, None] - position[None, :]
    angle = math.pi / count * offset.astype(jnp.float32)
    safe_sin = jnp.where(offset == 0, 1.0, jnp.sin(angle))
    parity = 1.0 - 2.0 * jnp.mod(offset, 2).astype(jnp.float32)
    return jnp.where(offset == 0, 0.0, 0.5 * FREQUENCY * parity * jnp.cos(angle) / safe_sin)


def euler_flux(fields, direction):
    density = fields[:, 0]
    momentum_x = fields[:, 1]
    momentum_y = fields[:, 2]
    momentum_z = fields[:, 3]
    energy = fields[:, 4]
    pressure = GAMMA_MINUS * (
        energy
        - 0.5
        * (momentum_x * momentum_x + momentum_y * momentum_y + momentum_z * momentum_z)
        / density
    )
    velocity = fields[:, direction] / density
    parts = [
        fields[:, direction],
        momentum_x * velocity,
        momentum_y * velocity,
        momentum_z * velocity,
        (energy + pressure) * velocity,
    ]
    parts[direction] = parts[direction] + pressure
    return jnp.stack(parts, axis=1)


def edge_rows(state, my_rows):
    low = state[:, :, :, 0:2]
    upper = lax.dynamic_slice_in_dim(state[:, :, 0], my_rows[0] - 2, 2, 2)
    highs = [upper[:, :, ::-1]]
    high = jnp.stack(highs, axis=2)
    return jnp.stack([low, high], axis=3)


def pick_ghosts(all_rims, local_slot, nb_side, shift):
    faces = []
    for face in range(2):
        taken = lax.dynamic_index_in_dim(all_rims, local_slot[0, face], 2, keepdims=False)
        taken = lax.dynamic_index_in_dim(taken, nb_side[0, face], 2, keepdims=False)
        faces.append(jnp.roll(taken, -shift[0, face], axis=3))
    per_block = [jnp.stack(faces, axis=2)]
    return jnp.stack(per_block, axis=2)


def spatial_residual(fields, ghosts, block_rows):
    row_count = fields.shape[3]
    stacked = jnp.concatenate([ghosts[:, :, :, 0, ::-1], fields, fields[:, :, :, -2:]], axis=3)
    offset = jnp.arange(row_count + 4, dtype=jnp.int32)[None, :] - 2 - block_rows[:, None]
    first_layer = (offset == 0)[None, None, :, :, None]
    second_layer = (offset == 1)[None, None, :, :, None]
    extended = jnp.where(
        first_layer,
        ghosts[:, :, :, 1, 0][:, :, :, None],
        jnp.where(second_layer, ghosts[:, :, :, 1, 1][:, :, :, None], stacked),
    )
    flux_rows = euler_flux(extended, 1)
    slope_rows = (
        8.0 * (flux_rows[:, :, :, 3:-1] - flux_rows[:, :, :, 1:-3])
        - (flux_rows[:, :, :, 4:] - flux_rows[:, :, :, :-4])
    ) / 12.0
    smooth_rows = (
        extended[:, :, :, 4:]
        - 4.0 * extended[:, :, :, 3:-1]
        + 6.0 * extended[:, :, :, 2:-2]
        - 4.0 * extended[:, :, :, 1:-3]
        + extended[:, :, :, :-4]
    )
    flux_cols = euler_flux(fields, 2)
    slope_cols = (
        8.0 * (jnp.roll(flux_cols, -1, 4) - jnp.roll(flux_cols, 1, 4))
        - (jnp.roll(flux_cols, -2, 4) - jnp.roll(flux_cols, 2, 4))
    ) / 12.0
    smooth_cols = (
        jnp.roll(fields, -2, 4)
        - 4.0 * jnp.roll(fields, -1, 4)
        + 6.0 * fields
        - 4.0 * jnp.roll(fields, 1, 4)
        + jnp.roll(fields, 2, 4)
    )
    return -(slope_rows + slope_cols) - DAMPING * (smooth_rows + smooth_cols)


def on_device(state, slot_of, conn_block, conn_side, conn_shift, rows):
    inst_dev = state.shape[0]
    blk_dev = state.shape[2]
    row_count = state.shape[3]
    blocks = slot_of.shape[0]
    ids_of_slot = (
        jnp.zeros((blocks,), jnp.int32).at[slot_of].set(jnp.arange(blocks, dtype=jnp.int32))
    )
    blk_place = lax.axis_index("blk")
    my_slots = blk_place * blk_dev + jnp.arange(blk_dev, dtype=jnp.int32)
    my_ids = ids_of_slot[my_slots]
    my_rows = rows[my_ids]
    boundary = edge_rows(state, my_rows)
    nb_slots = slot_of[conn_block[my_ids]]
    blk_span = lax.axis_size("blk")
    pieces = []
    for window in range(2 * REACH + 1):
        if window == REACH:
            pieces.append(boundary)
        else:
            pieces.append(passed_along(boundary, "blk", REACH - window))
    all_rims = jnp.concatenate(pieces, axis=2)
    distance = jnp.mod(nb_slots // blk_dev - blk_place + REACH, blk_span)
    local_slot = distance * blk_dev + jnp.mod(nb_slots, blk_dev)
    ghosts = pick_ghosts(all_rims, local_slot, conn_side[my_ids], conn_shift[my_ids])
    spatial = spatial_residual(state, ghosts, my_rows)
    cycle_size = lax.axis_size("inst")
    cycle_place = lax.axis_index("inst")
    derivative = spectral_matrix(inst_dev * cycle_size)
    own_rows = lax.dynamic_slice_in_dim(derivative, cycle_place * inst_dev, inst_dev, 0)
    all_states = lax.all_gather(state, "inst", axis=0, tiled=True)
    source = jnp.einsum("nm,mvbij->nvbij", own_rows, all_states, precision=lax.Precision.HIGHEST)
    inside = (jnp.arange(row_count, dtype=jnp.int32)[None, :] < my_rows[:, None])[
        None, None, :, :, None
    ]
    return jnp.where(inside, spatial - source, 0.0)


def solution(mesh):
    in_specs = (P("inst", None, "blk", None, None), P(), P(), P(), P(), P())
    out_specs = P("inst", None, "blk", None, None)
    return jax.shard_map(
        on_device, mesh=mesh, in_specs=in_specs, out_specs=out_specs, check_vma=False
    )
```

profile of v0, /device:TPU:9, one launch (start us, length us, event | category | flops | bytes accessed | tf_op | source)
XLA Modules:
  0.0 100.9 jit_solution(9239169802677168952)
XLA Ops:
  6.6 0.7 compare_select_fusion
  7.3 1.4 %scatter_custom_fusion = s32[256]{0:T(256)S(1)} fusion(s32[256]{0:T(256)S(1)} %compare_select_fusion, s32[256]{0:T(256)S(1)} %iota.25, s32[]{:T(128)} %constant.170.clone.1), kind=kCustom, calls=%fused_computation.104 | custom fusion | bytes 1028 | tf_op jit(solution)/shard_map/scatter | solution.py:114
  8.7 0.7 dynamic-slice.18
  11.5 1.3 %dynamic-slice.19 = s32[1]{0:T(128)} dynamic-slice(s32[256]{0:T(256)} %param.13, s32[]{:T(128)} %bitcast.2), dynamic_slice_sizes={1} | dynamic-slice | bytes 12 | tf_op jit(solution)/shard_map/gather | solution.py:119
  13.9 1.0 %slice_bitcast_fusion = (f32[4,5,1,1,2,256]{5,4,1,0,3,2:T(2,128)S(1)}, f32[4,5,2,256]{3,2,1,0:T(2,128)S(1)}) fusion(f32[4,5,1,32,256]{4,3,2,1,0:T(8,128)} %param.8, s32[]{:T(128)S(6)} %select_n.131), kind=kLoop, calls=%fused_computation.65 | loop fusion | bytes 163844 | tf_op jit(solution)/shard_map/stack | solution.py:57
  15.2 3.2 %collective-permute-start = (f32[4,5,1,2,2,256]{5,4,1,0,3,2:T(2,128)S(1)}, f32[4,5,1,2,2,256]{5,4,1,0,3,2:T(2,128)S(1)}, u32[]{:S(2)}, u32[]{:S(2)}) collective-permute-start(f32[4,5,1,2,2,256]{5,4,1,0,3,2:T(2,128)S(1)} %pad_maximum_fusion), channel_id=1, source_target_pairs={{0,2},{1,3},{2,4},{3,5},{4,6},{5,7},{6,8},{7,9},{8,10},{9,11},{10,... | collective-permute-start | bytes 245768 | tf_op jit(solution)/shard_map/ppermute | solution.py:16
  18.4 3.9 %collective-permute-start.1 = (f32[4,5,1,2,2,256]{5,4,1,0,3,2:T(2,128)S(1)}, f32[4,5,1,2,2,256]{5,4,1,0,3,2:T(2,128)S(1)}, u32[]{:S(2)}, u32[]{:S(2)}) collective-permute-start(f32[4,5,1,2,2,256]{5,4,1,0,3,2:T(2,128)S(1)} %pad_maximum_fusion), channel_id=1, source_target_pairs={{0,1},{1,2},{2,3},{3,4},{4,5},{5,6},{6,7},{7,8},{8,9},{9,10},{10,1... | collective-permute-start | bytes 245768 | tf_op jit(solution)/shard_map/ppermute | solution.py:16
  22.3 1.9 %collective-permute-start.2 = (f32[4,5,1,2,2,256]{5,4,1,0,3,2:T(2,128)S(1)}, f32[4,5,1,2,2,256]{5,4,1,0,3,2:T(2,128)S(1)}, u32[]{:S(2)}, u32[]{:S(2)}) collective-permute-start(f32[4,5,1,2,2,256]{5,4,1,0,3,2:T(2,128)S(1)} %pad_maximum_fusion), channel_id=1, source_target_pairs={{0,255},{1,0},{2,1},{3,2},{4,3},{5,4},{6,5},{7,6},{8,7},{9,8},{10,... | collective-permute-start | bytes 245768 | tf_op jit(solution)/shard_map/ppermute | solution.py:16
  24.2 4.3 %collective-permute-start.3 = (f32[4,5,1,2,2,256]{5,4,1,0,3,2:T(2,128)S(1)}, f32[4,5,1,2,2,256]{5,4,1,0,3,2:T(2,128)S(1)}, u32[]{:S(2)}, u32[]{:S(2)}) collective-permute-start(f32[4,5,1,2,2,256]{5,4,1,0,3,2:T(2,128)S(1)} %pad_maximum_fusion), channel_id=1, source_target_pairs={{0,254},{1,255},{2,0},{3,1},{4,2},{5,3},{6,4},{7,5},{8,6},{9,7},{1... | collective-permute-start | bytes 245768 | tf_op jit(solution)/shard_map/ppermute | solution.py:16
  29.4 0.7 fusion.62
  39.7 1.5 %fusion.59 = (f32[4,5,1,32,255]{4,0,3,1,2:T(4,128)}, f32[4,5,1,32,255]{4,0,3,1,2:T(4,128)}) fusion(f32[4,5,1,32,256]{4,0,3,1,2:T(4,128)S(1)} %multiply_dynamic-update-slice_fusion.3), kind=kLoop, calls=%fused_computation.116 | loop fusion | bytes 2611200 | tf_op jit(solution)/shard_map/jit(_roll_static)/slice | solution.py:95
  41.3 1.1 %fusion.56 = (f32[4,5,1,32,2]{4,0,3,1,2:T(4,128)}, f32[4,5,1,32,2]{4,0,3,1,2:T(4,128)}) fusion(f32[4,5,1,32,256]{4,0,3,1,2:T(4,128)S(1)} %multiply_dynamic-update-slice_fusion.3), kind=kLoop, calls=%fused_computation.113 | loop fusion | bytes 20480 | tf_op jit(solution)/shard_map/jit(_roll_static)/slice | solution.py:96
  42.3 1.0 %fusion.58 = (f32[4,5,1,32,1]{4,0,3,1,2:T(4,128)}, f32[4,5,1,32,1]{4,0,3,1,2:T(4,128)}) fusion(f32[4,5,1,32,256]{4,0,3,1,2:T(4,128)S(1)} %multiply_dynamic-update-slice_fusion.3), kind=kLoop, calls=%fused_computation.115 | loop fusion | bytes 10240 | tf_op jit(solution)/shard_map/jit(_roll_static)/slice | solution.py:95
  43.3 1.5 %fusion.53 = (f32[4,5,1,32,254]{4,0,3,1,2:T(4,128)}, f32[4,5,1,32,254]{4,0,3,1,2:T(4,128)}) fusion(f32[4,5,1,32,256]{4,0,3,1,2:T(4,128)S(1)} %copy.48), kind=kLoop, calls=%fused_computation.110 | loop fusion | bytes 2600960 | tf_op jit(solution)/shard_map/jit(_roll_static)/slice | solution.py:103
  44.9 1.5 %fusion.55 = (f32[4,5,1,32,255]{4,0,3,1,2:T(4,128)}, f32[4,5,1,32,255]{4,0,3,1,2:T(4,128)}) fusion(f32[4,5,1,32,256]{4,0,3,1,2:T(4,128)S(1)} %copy.48), kind=kLoop, calls=%fused_computation.112 | loop fusion | bytes 2611200 | tf_op jit(solution)/shard_map/jit(_roll_static)/slice | solution.py:102
  46.4 1.1 %fusion.52 = (f32[4,5,1,32,2]{4,0,3,1,2:T(4,128)}, f32[4,5,1,32,2]{4,0,3,1,2:T(4,128)}) fusion(f32[4,5,1,32,256]{4,0,3,1,2:T(4,128)S(1)} %copy.48), kind=kLoop, calls=%fused_computation.109 | loop fusion | bytes 20480 | tf_op jit(solution)/shard_map/jit(_roll_static)/slice | solution.py:103
  47.5 1.1 %fusion.54 = (f32[4,5,1,32,1]{4,0,3,1,2:T(4,128)}, f32[4,5,1,32,1]{4,0,3,1,2:T(4,128)}) fusion(f32[4,5,1,32,256]{4,0,3,1,2:T(4,128)S(1)} %copy.48), kind=kLoop, calls=%fused_computation.111 | loop fusion | bytes 10240 | tf_op jit(solution)/shard_map/jit(_roll_static)/slice | solution.py:102
  53.5 0.8 add_dynamic-update-slice_fusion
  54.2 0.7 multiply_dynamic-update-slice_fusion.2
  54.9 0.7 multiply_dynamic-update-slice_fusion.1
  55.6 0.7 multiply_dynamic-update-slice_fusion
  56.4 29.0 %all-gather.2.cloned.1.call-done = f32[8,5,1,32,256]{4,3,2,1,0:T(8,128)} async-done(((f32[4,5,1,32,256]{4,3,2,1,0:T(8,128)}), f32[8,5,1,32,256]{4,3,2,1,0:T(8,128)}) %all-gather.2.cloned.1.call-update) | async-done | bytes 1310736 | tf_op jit(solution)/shard_map/all_gather | solution.py:138
  85.4 7.7 %fusion.9 = f32[4,5,1,32,256]{4,0,3,1,2:T(4,128)S(1)} fusion(f32[8,5,1,32,256]{4,3,2,1,0:T(8,128)} %all-gather.2.cloned.1.call-done, f32[4,5,1,36,256]{4,0,3,1,2:T(4,128)S(1)} %fusion.12, f32[4,5,1,36,256]{4,0,3,1,2:T(4,128)} %multiply_dynamic-update-slice_fusion, f32[4,5,1,32,1]{4,0,3,1,2:T(4,128)} %get-tuple-element.81, ...), kind=kOutput, calls=%fused_computation.7 | convolution fusion | flops 21954560 | bytes 13775364 | tf_op jit(solution)/shard_map/nm,mvbij->nvbij/dot_general | solution.py:139
  93.1 1.0 copy.64
  (59 shorter events, 6.3 us)
Async XLA Ops:
  6.5 22.0 %copy-start = (s32[256,2]{0,1:T(2,128)S(1)}, s32[256,2]{0,1:T(2,128)}, u32[]{:S(2)}) copy-start(s32[256,2]{0,1:T(2,128)} %param.10) | copy-start | bytes 6148
  6.5 22.2 %copy-start.1 = (s32[256]{0:T(256)S(1)}, s32[256]{0:T(256)}, u32[]{:S(2)}) copy-start(s32[256]{0:T(256)} %param.9) | copy-start | bytes 3076
  6.5 31.9 %copy-start.4 = (f32[4,5,1,32,256]{4,3,2,1,0:T(8,128)S(1)}, f32[4,5,1,32,256]{4,3,2,1,0:T(8,128)}, u32[]{:S(2)}) copy-start(f32[4,5,1,32,256]{4,3,2,1,0:T(8,128)} %param.8) | copy-start | bytes 1966084
  6.5 26.1 %copy-start.6 = (s32[256,2]{0,1:T(2,128)S(1)}, s32[256,2]{0,1:T(2,128)}, u32[]{:S(2)}) copy-start(s32[256,2]{0,1:T(2,128)} %param.11) | copy-start | bytes 6148
  6.5 26.1 %copy-start.5 = (s32[256,2]{0,1:T(2,128)S(1)}, s32[256,2]{0,1:T(2,128)}, u32[]{:S(2)}) copy-start(s32[256,2]{0,1:T(2,128)} %param.12) | copy-start | bytes 6148
  6.5 78.8 %all-gather.2.cloned.1.call-start = ((), (), s32[]{:S(2)}) async-start(), calls=%async_computation | async-start | bytes 1966080 | tf_op jit(solution)/shard_map/all_gather | solution.py:138
  15.2 36.7 %collective-permute-start = (f32[4,5,1,2,2,256]{5,4,1,0,3,2:T(2,128)S(1)}, f32[4,5,1,2,2,256]{5,4,1,0,3,2:T(2,128)S(1)}, u32[]{:S(2)}, u32[]{:S(2)}) collective-permute-start(f32[4,5,1,2,2,256]{5,4,1,0,3,2:T(2,128)S(1)} %pad_maximum_fusion), channel_id=1, source_target_pairs={{0,2},{1,3},{2,4},{3,5},{4,6},{5,7},{6,8},{7,9},{8,10},{9,11},{10,... | collective-permute-start | bytes 245768 | tf_op jit(solution)/shard_map/ppermute | solution.py:16
  18.4 33.5 %collective-permute-start.1 = (f32[4,5,1,2,2,256]{5,4,1,0,3,2:T(2,128)S(1)}, f32[4,5,1,2,2,256]{5,4,1,0,3,2:T(2,128)S(1)}, u32[]{:S(2)}, u32[]{:S(2)}) collective-permute-start(f32[4,5,1,2,2,256]{5,4,1,0,3,2:T(2,128)S(1)} %pad_maximum_fusion), channel_id=1, source_target_pairs={{0,1},{1,2},{2,3},{3,4},{4,5},{5,6},{6,7},{7,8},{8,9},{9,10},{10,1... | collective-permute-start | bytes 245768 | tf_op jit(solution)/shard_map/ppermute | solution.py:16
  22.3 29.7 %collective-permute-start.2 = (f32[4,5,1,2,2,256]{5,4,1,0,3,2:T(2,128)S(1)}, f32[4,5,1,2,2,256]{5,4,1,0,3,2:T(2,128)S(1)}, u32[]{:S(2)}, u32[]{:S(2)}) collective-permute-start(f32[4,5,1,2,2,256]{5,4,1,0,3,2:T(2,128)S(1)} %pad_maximum_fusion), channel_id=1, source_target_pairs={{0,255},{1,0},{2,1},{3,2},{4,3},{5,4},{6,5},{7,6},{8,7},{9,8},{10,... | collective-permute-start | bytes 245768 | tf_op jit(solution)/shard_map/ppermute | solution.py:16
  24.2 27.8 %collective-permute-start.3 = (f32[4,5,1,2,2,256]{5,4,1,0,3,2:T(2,128)S(1)}, f32[4,5,1,2,2,256]{5,4,1,0,3,2:T(2,128)S(1)}, u32[]{:S(2)}, u32[]{:S(2)}) collective-permute-start(f32[4,5,1,2,2,256]{5,4,1,0,3,2:T(2,128)S(1)} %pad_maximum_fusion), channel_id=1, source_target_pairs={{0,254},{1,255},{2,0},{3,1},{4,2},{5,3},{6,4},{7,5},{8,6},{9,7},{1... | collective-permute-start | bytes 245768 | tf_op jit(solution)/shard_map/ppermute | solution.py:16
  38.9 8.5 %copy-start.2 = (f32[4,5,1,32,256]{4,0,3,1,2:T(4,128)}, f32[4,5,1,32,256]{4,0,3,1,2:T(4,128)S(1)}, u32[]{:S(2)}) copy-start(f32[4,5,1,32,256]{4,0,3,1,2:T(4,128)S(1)} %copy.48) | copy-start | bytes 1966084
  48.5 4.0 %copy-start.3 = (f32[4,5,1,32,256]{4,0,3,1,2:T(4,128)S(1)}, f32[4,5,1,32,256]{4,0,3,1,2:T(4,128)}, u32[]{:S(2)}) copy-start(f32[4,5,1,32,256]{4,0,3,1,2:T(4,128)} %copy-done.2) | copy-start | bytes 1966084
  48.6 4.0 %slice-start = ((f32[4,5,1,32,256]{4,0,3,1,2:T(4,128)}), f32[4,5,1,2,256]{4,0,3,1,2:T(4,128)S(1)}, s32[]{:S(2)}) async-start(f32[4,5,1,32,256]{4,0,3,1,2:T(4,128)} %copy-done.2), calls=%async_computation.1 | async-start | bytes 81920 | tf_op jit(solution)/shard_map/slice | solution.py:72
Sparse Core Ops, SparseCore 0:
  28.7 56.6 all-gather.1
where the time goes:
time: 101 us
  waiting for transfers between devices  29 us (29%)
  between operations  26.1 us (26%)
  local copies, waits for them, and re-layouts  18.7 us (19%)
  starting transfers between devices  13.4 us (13%)
  matrix products  7.73 us (8%)
  other arithmetic  5.89 us (6%)
    all_gather x1, waiting for transfers between devices, on_device(): all_states = lax.all_gather(state, 'inst', axis=0, tiled=True)  29 us
    ppermute x4, starting transfers between devices, passed_along(): return lax.ppermute(value, axis, pairs)  13.3 us
    dot_general x1, matrix products, on_device(): jnp.einsum('nm,mvbij->nvbij', own_rows, all_states, precision=lax.Precisi...  7.73 us
    slice x2, local copies, waits for them, and re-layouts, spatial_residual(): jnp.roll(fields, 1, 4)  2.62 us
    slice x2, local copies, waits for them, and re-layouts, spatial_residual(): jnp.roll(fields, 2, 4)  2.58 us
    slice x2, local copies, waits for them, and re-layouts, spatial_residual(): jnp.roll(flux_cols, 1, 4)  2.56 us
    unnamed x7, other arithmetic  2.49 us
  transfers between devices with their start and end apart: 5, of which 1 were waited for; matrix products, arithmetic and copies ran while one was open for 18% of the time, Pallas kernels for 0%

commit v1 on v0

--- a/solution.py
+++ b/solution.py
@@ -135,7 +135,10 @@
     cycle_place = lax.axis_index("inst")
     derivative = spectral_matrix(inst_dev * cycle_size)
     own_rows = lax.dynamic_slice_in_dim(derivative, cycle_place * inst_dev, inst_dev, 0)
-    all_states = lax.all_gather(state, "inst", axis=0, tiled=True)
+    size = lax.axis_size("inst")
+    shards = jnp.stack([state for _ in range(size)])
+    shards = lax.all_to_all(shards, "inst", split_axis=0, concat_axis=0)
+    all_states = jnp.concatenate(shards, axis=0)
     source = jnp.einsum("nm,mvbij->nvbij", own_rows, all_states, precision=lax.Precision.HIGHEST)
     inside = (jnp.arange(row_count, dtype=jnp.int32)[None, :] < my_rows[:, None])[
         None, None, :, :, None

time: 101 us -> 77.6 us (0.77)
  the two profiles are of different devices: /device:TPU:9 before, /device:TPU:32 now
where the time goes in v1:
time: 77.6 us; the launch traced here: 77.1 us
  starting transfers between devices  28.4 us (37%)
  local copies, waits for them, and re-layouts  20 us (26%)
  between operations  12.7 us (16%)
  other arithmetic  8.64 us (11%)
  matrix products  7.41 us (10%)
    ppermute x4, starting transfers between devices, passed_along(): return lax.ppermute(value, axis, pairs)  21 us
    dot_general x1, matrix products, on_device(): jnp.einsum('nm,mvbij->nvbij', own_rows, all_states, precision=lax.Precisi...  7.41 us
    all_to_all x1, starting transfers between devices, on_device(): shards = lax.all_to_all(shards, 'inst', split_axis=0, concat_axis=0)  7.33 us
    slice x2, local copies, waits for them, and re-layouts, spatial_residual(): jnp.roll(flux_cols, 2, 4)  2.62 us
    slice x2, local copies, waits for them, and re-layouts, spatial_residual(): jnp.roll(fields, 2, 4)  2.62 us
    slice x2, local copies, waits for them, and re-layouts, spatial_residual(): jnp.roll(flux_cols, 1, 4)  2.59 us
    slice x2, local copies, waits for them, and re-layouts, spatial_residual(): jnp.roll(fields, 1, 4)  2.54 us
    another operation x1, other arithmetic, on_device(): shards = jnp.stack([state for _ in range(size)])  2.54 us
  transfers between devices with their start and end apart: 5, of which 0 were waited for; matrix products, arithmetic and copies ran while one was open for 29% of the time, Pallas kernels for 0%

profile of v1, /device:TPU:32, one launch (start us, length us, event | category | flops | bytes accessed | tf_op | source)
XLA Modules:
  0.0 77.1 jit_solution(13649855710008456810)
XLA Ops:
  0.7 1.4 %scatter_custom_fusion = s32[256]{0:T(256)S(1)} fusion(s32[256]{0:T(256)S(1)} %compare_select_fusion, s32[256]{0:T(256)S(1)} %iota.25, s32[]{:T(128)} %constant.170.clone.1), kind=kCustom, calls=%fused_computation.104 | custom fusion | bytes 1028 | tf_op jit(solution)/shard_map/scatter | solution.py:114
  4.8 1.3 %dynamic-slice.19 = s32[1]{0:T(128)} dynamic-slice(s32[256]{0:T(256)} %param.13, s32[]{:T(128)} %bitcast.2), dynamic_slice_sizes={1} | dynamic-slice | bytes 12 | tf_op jit(solution)/shard_map/gather | solution.py:119
  7.6 1.0 %slice_bitcast_fusion = (f32[4,5,1,1,2,256]{5,4,1,0,3,2:T(2,128)S(1)}, f32[4,5,2,256]{3,2,1,0:T(2,128)S(1)}) fusion(f32[4,5,1,32,256]{4,3,2,1,0:T(8,128)} %param.8, s32[]{:T(128)S(6)} %select_n.131), kind=kLoop, calls=%fused_computation.65 | loop fusion | bytes 163844 | tf_op jit(solution)/shard_map/stack | solution.py:57
  8.8 3.5 %collective-permute-start = (f32[4,5,1,2,2,256]{5,4,1,0,3,2:T(2,128)S(1)}, f32[4,5,1,2,2,256]{5,4,1,0,3,2:T(2,128)S(1)}, u32[]{:S(2)}, u32[]{:S(2)}) collective-permute-start(f32[4,5,1,2,2,256]{5,4,1,0,3,2:T(2,128)S(1)} %pad_maximum_fusion.1), channel_id=1, source_target_pairs={{0,2},{1,3},{2,4},{3,5},{4,6},{5,7},{6,8},{7,9},{8,10},{9,11},{10,... | collective-permute-start | bytes 245768 | tf_op jit(solution)/shard_map/ppermute | solution.py:16
  12.3 1.9 %collective-permute-start.1 = (f32[4,5,1,2,2,256]{5,4,1,0,3,2:T(2,128)S(1)}, f32[4,5,1,2,2,256]{5,4,1,0,3,2:T(2,128)S(1)}, u32[]{:S(2)}, u32[]{:S(2)}) collective-permute-start(f32[4,5,1,2,2,256]{5,4,1,0,3,2:T(2,128)S(1)} %pad_maximum_fusion.1), channel_id=1, source_target_pairs={{0,1},{1,2},{2,3},{3,4},{4,5},{5,6},{6,7},{7,8},{8,9},{9,10},{10,1... | collective-permute-start | bytes 245768 | tf_op jit(solution)/shard_map/ppermute | solution.py:16
  14.3 11.4 %collective-permute-start.2 = (f32[4,5,1,2,2,256]{5,4,1,0,3,2:T(2,128)S(1)}, f32[4,5,1,2,2,256]{5,4,1,0,3,2:T(2,128)S(1)}, u32[]{:S(2)}, u32[]{:S(2)}) collective-permute-start(f32[4,5,1,2,2,256]{5,4,1,0,3,2:T(2,128)S(1)} %pad_maximum_fusion.1), channel_id=1, source_target_pairs={{0,255},{1,0},{2,1},{3,2},{4,3},{5,4},{6,5},{7,6},{8,7},{9,8},{10,... | collective-permute-start | bytes 245768 | tf_op jit(solution)/shard_map/ppermute | solution.py:16
  25.7 4.2 %collective-permute-start.3 = (f32[4,5,1,2,2,256]{5,4,1,0,3,2:T(2,128)S(1)}, f32[4,5,1,2,2,256]{5,4,1,0,3,2:T(2,128)S(1)}, u32[]{:S(2)}, u32[]{:S(2)}) collective-permute-start(f32[4,5,1,2,2,256]{5,4,1,0,3,2:T(2,128)S(1)} %pad_maximum_fusion.1), channel_id=1, source_target_pairs={{0,254},{1,255},{2,0},{3,1},{4,2},{5,3},{6,4},{7,5},{8,6},{9,7},{1... | collective-permute-start | bytes 245768 | tf_op jit(solution)/shard_map/ppermute | solution.py:16
  29.9 2.5 %pad_maximum_fusion = f32[2,4,5,1,32,256]{5,4,2,1,3,0:T(8,128)} fusion(f32[1,4,5,1,32,256]{5,4,2,1,3,0:T(8,128)} %bitcast.52), kind=kLoop, calls=%fused_computation.2 | loop fusion | flops 327680 | bytes 1966080 | tf_op jit(solution)/shard_map/stack | solution.py:139
  32.5 7.3 %all-to-all-start = ((f32[2,4,5,1,32,256]{5,4,2,1,3,0:T(8,128)}), f32[2,4,5,1,32,256]{5,4,2,1,3,0:T(8,128)S(1)}, u32[]{:S(2)}, u32[]{:S(2)}) async-start(f32[2,4,5,1,32,256]{5,4,2,1,3,0:T(8,128)} %pad_maximum_fusion), calls=%async_computation | async-start | bytes 2621440 | tf_op jit(solution)/shard_map/all_to_all | solution.py:140
  49.4 0.7 fusion.49
  50.4 1.1 %fusion.57 = (f32[4,5,1,32,1]{4,0,3,1,2:T(4,128)}, f32[4,5,1,32,1]{4,0,3,1,2:T(4,128)}) fusion(f32[4,5,1,32,256]{4,0,3,1,2:T(4,128)S(1)} %multiply_dynamic-update-slice_fusion.3), kind=kLoop, calls=%fused_computation.115 | loop fusion | bytes 10240 | tf_op jit(solution)/shard_map/jit(_roll_static)/slice | solution.py:95
  51.5 1.5 %fusion.58 = (f32[4,5,1,32,255]{4,0,3,1,2:T(4,128)}, f32[4,5,1,32,255]{4,0,3,1,2:T(4,128)}) fusion(f32[4,5,1,32,256]{4,0,3,1,2:T(4,128)S(1)} %multiply_dynamic-update-slice_fusion.3), kind=kLoop, calls=%fused_computation.116 | loop fusion | bytes 2611200 | tf_op jit(solution)/shard_map/jit(_roll_static)/slice | solution.py:95
  53.0 1.1 %fusion.55 = (f32[4,5,1,32,2]{4,0,3,1,2:T(4,128)}, f32[4,5,1,32,2]{4,0,3,1,2:T(4,128)}) fusion(f32[4,5,1,32,256]{4,0,3,1,2:T(4,128)S(1)} %multiply_dynamic-update-slice_fusion.3), kind=kLoop, calls=%fused_computation.113 | loop fusion | bytes 20480 | tf_op jit(solution)/shard_map/jit(_roll_static)/slice | solution.py:96
  54.1 1.5 %fusion.56 = (f32[4,5,1,32,254]{4,0,3,1,2:T(4,128)}, f32[4,5,1,32,254]{4,0,3,1,2:T(4,128)}) fusion(f32[4,5,1,32,256]{4,0,3,1,2:T(4,128)S(1)} %multiply_dynamic-update-slice_fusion.3), kind=kLoop, calls=%fused_computation.114 | loop fusion | bytes 2600960 | tf_op jit(solution)/shard_map/jit(_roll_static)/slice | solution.py:96
  55.7 1.1 %fusion.51 = (f32[4,5,1,32,2]{4,0,3,1,2:T(4,128)}, f32[4,5,1,32,2]{4,0,3,1,2:T(4,128)}) fusion(f32[4,5,1,32,256]{4,0,3,1,2:T(4,128)S(1)} %copy.28), kind=kLoop, calls=%fused_computation.109 | loop fusion | bytes 20480 | tf_op jit(solution)/shard_map/jit(_roll_static)/slice | solution.py:103
  56.7 1.5 %fusion.52 = (f32[4,5,1,32,254]{4,0,3,1,2:T(4,128)}, f32[4,5,1,32,254]{4,0,3,1,2:T(4,128)}) fusion(f32[4,5,1,32,256]{4,0,3,1,2:T(4,128)S(1)} %copy.28), kind=kLoop, calls=%fused_computation.110 | loop fusion | bytes 2600960 | tf_op jit(solution)/shard_map/jit(_roll_static)/slice | solution.py:103
  58.3 1.0 %fusion.53 = (f32[4,5,1,32,1]{4,0,3,1,2:T(4,128)}, f32[4,5,1,32,1]{4,0,3,1,2:T(4,128)}) fusion(f32[4,5,1,32,256]{4,0,3,1,2:T(4,128)S(1)} %copy.28), kind=kLoop, calls=%fused_computation.111 | loop fusion | bytes 10240 | tf_op jit(solution)/shard_map/jit(_roll_static)/slice | solution.py:102
  59.3 1.5 %fusion.54 = (f32[4,5,1,32,255]{4,0,3,1,2:T(4,128)}, f32[4,5,1,32,255]{4,0,3,1,2:T(4,128)}) fusion(f32[4,5,1,32,256]{4,0,3,1,2:T(4,128)S(1)} %copy.28), kind=kLoop, calls=%fused_computation.112 | loop fusion | bytes 2611200 | tf_op jit(solution)/shard_map/jit(_roll_static)/slice | solution.py:102
  65.8 0.8 %add_dynamic-update-slice_fusion = (f32[4,5,1,36,256]{4,0,3,1,2:T(4,128)}, f32[4,1,1,36,256]{4,0,3,1,2:T(4,128)S(1)}, f32[4,1,1,36,256]{4,0,3,1,2:T(4,128)S(1)}) fusion(f32[4,5,1,36,256]{4,0,3,1,2:T(4,128)} %slice_dynamic-update-slice_fusion, f32[4,5,1,36,256]{4,0,3,1,2:T(4,128)S(1)} %fusion.11), kind=kLoop, calls=%fused_computation.40 | loop fusion | flops 442368 | bytes 1179648
  66.6 0.7 multiply_dynamic-update-slice_fusion.2
  67.3 0.7 multiply_dynamic-update-slice_fusion.1
  68.0 0.7 multiply_dynamic-update-slice_fusion
  68.7 7.4 %fusion.8 = f32[4,5,1,32,256]{4,0,3,1,2:T(4,128)S(1)} fusion(f32[8,5,32,256]{3,2,1,0:T(8,128)S(1)} %bitcast.53, f32[4,5,1,36,256]{4,0,3,1,2:T(4,128)S(1)} %fusion.11, f32[4,5,1,36,256]{4,0,3,1,2:T(4,128)} %multiply_dynamic-update-slice_fusion, f32[4,5,1,32,1]{4,0,3,1,2:T(4,128)} %get-tuple-element.81, f32[4,5,1,32,255]{4,0,3,1,2:T(4,128)} %get-tuple-element.83, ...), kind=kOutput, calls=%fused_computation.7 | convolution fusion | flops 21954560 | bytes 13765124 | tf_op jit(solution)/shard_map/nm,mvbij->nvbij/dot_general | solution.py:142
  76.1 1.0 %copy.44 = f32[4,5,1,32,256]{4,3,2,1,0:T(8,128)} copy(f32[4,5,1,32,256]{4,0,3,1,2:T(4,128)S(1)} %fusion.8) | data formatting | bytes 1310720 | tf_op jit(solution)/shard_map/jit(_where)/select_n | solution.py:146
  (59 shorter events, 7.4 us)
Async XLA Ops:
  0.0 41.6 %copy-start = (s32[256,2]{0,1:T(2,128)S(1)}, s32[256,2]{0,1:T(2,128)}, u32[]{:S(2)}) copy-start(s32[256,2]{0,1:T(2,128)} %param.10) | copy-start | bytes 6148
  8.8 55.3 %collective-permute-start = (f32[4,5,1,2,2,256]{5,4,1,0,3,2:T(2,128)S(1)}, f32[4,5,1,2,2,256]{5,4,1,0,3,2:T(2,128)S(1)}, u32[]{:S(2)}, u32[]{:S(2)}) collective-permute-start(f32[4,5,1,2,2,256]{5,4,1,0,3,2:T(2,128)S(1)} %pad_maximum_fusion.1), channel_id=1, source_target_pairs={{0,2},{1,3},{2,4},{3,5},{4,6},{5,7},{6,8},{7,9},{8,10},{9,11},{10,... | collective-permute-start | bytes 245768 | tf_op jit(solution)/shard_map/ppermute | solution.py:16
  12.3 51.9 %collective-permute-start.1 = (f32[4,5,1,2,2,256]{5,4,1,0,3,2:T(2,128)S(1)}, f32[4,5,1,2,2,256]{5,4,1,0,3,2:T(2,128)S(1)}, u32[]{:S(2)}, u32[]{:S(2)}) collective-permute-start(f32[4,5,1,2,2,256]{5,4,1,0,3,2:T(2,128)S(1)} %pad_maximum_fusion.1), channel_id=1, source_target_pairs={{0,1},{1,2},{2,3},{3,4},{4,5},{5,6},{6,7},{7,8},{8,9},{9,10},{10,1... | collective-permute-start | bytes 245768 | tf_op jit(solution)/shard_map/ppermute | solution.py:16
  14.3 50.0 %collective-permute-start.2 = (f32[4,5,1,2,2,256]{5,4,1,0,3,2:T(2,128)S(1)}, f32[4,5,1,2,2,256]{5,4,1,0,3,2:T(2,128)S(1)}, u32[]{:S(2)}, u32[]{:S(2)}) collective-permute-start(f32[4,5,1,2,2,256]{5,4,1,0,3,2:T(2,128)S(1)} %pad_maximum_fusion.1), channel_id=1, source_target_pairs={{0,255},{1,0},{2,1},{3,2},{4,3},{5,4},{6,5},{7,6},{8,7},{9,8},{10,... | collective-permute-start | bytes 245768 | tf_op jit(solution)/shard_map/ppermute | solution.py:16
  25.7 38.6 %collective-permute-start.3 = (f32[4,5,1,2,2,256]{5,4,1,0,3,2:T(2,128)S(1)}, f32[4,5,1,2,2,256]{5,4,1,0,3,2:T(2,128)S(1)}, u32[]{:S(2)}, u32[]{:S(2)}) collective-permute-start(f32[4,5,1,2,2,256]{5,4,1,0,3,2:T(2,128)S(1)} %pad_maximum_fusion.1), channel_id=1, source_target_pairs={{0,254},{1,255},{2,0},{3,1},{4,2},{5,3},{6,4},{7,5},{8,6},{9,7},{1... | collective-permute-start | bytes 245768 | tf_op jit(solution)/shard_map/ppermute | solution.py:16
  32.5 7.3 %copy-start.4 = (f32[4,5,1,32,256]{4,3,2,1,0:T(8,128)S(1)}, f32[4,5,1,32,256]{4,3,2,1,0:T(8,128)}, u32[]{:S(2)}) copy-start(f32[4,5,1,32,256]{4,3,2,1,0:T(8,128)} %param.8) | copy-start | bytes 1966084
  32.5 7.8 %copy-start.5 = (s32[256,2]{0,1:T(2,128)S(1)}, s32[256,2]{0,1:T(2,128)}, u32[]{:S(2)}) copy-start(s32[256,2]{0,1:T(2,128)} %param.12) | copy-start | bytes 6148
  32.5 7.8 %copy-start.6 = (s32[256,2]{0,1:T(2,128)S(1)}, s32[256,2]{0,1:T(2,128)}, u32[]{:S(2)}) copy-start(s32[256,2]{0,1:T(2,128)} %param.11) | copy-start | bytes 6148
  32.5 36.2 %all-to-all-start = ((f32[2,4,5,1,32,256]{5,4,2,1,3,0:T(8,128)}), f32[2,4,5,1,32,256]{5,4,2,1,3,0:T(8,128)S(1)}, u32[]{:S(2)}, u32[]{:S(2)}) async-start(f32[2,4,5,1,32,256]{5,4,2,1,3,0:T(8,128)} %pad_maximum_fusion), calls=%async_computation | async-start | bytes 2621440 | tf_op jit(solution)/shard_map/all_to_all | solution.py:140
  39.8 2.0 %copy-start.1 = (s32[256]{0:T(256)S(1)}, s32[256]{0:T(256)}, u32[]{:S(2)}) copy-start(s32[256]{0:T(256)} %param.9) | copy-start | bytes 3076
  40.2 19.1 %copy-start.2 = (f32[4,5,1,32,256]{4,0,3,1,2:T(4,128)}, f32[4,5,1,32,256]{4,0,3,1,2:T(4,128)S(1)}, u32[]{:S(2)}) copy-start(f32[4,5,1,32,256]{4,0,3,1,2:T(4,128)S(1)} %copy.28) | copy-start | bytes 1966084
  60.8 4.0 %copy-start.3 = (f32[4,5,1,32,256]{4,0,3,1,2:T(4,128)S(1)}, f32[4,5,1,32,256]{4,0,3,1,2:T(4,128)}, u32[]{:S(2)}) copy-start(f32[4,5,1,32,256]{4,0,3,1,2:T(4,128)} %copy-done.2) | copy-start | bytes 1966084
  60.8 4.0 %slice-start = ((f32[4,5,1,32,256]{4,0,3,1,2:T(4,128)}), f32[4,5,1,2,256]{4,0,3,1,2:T(4,128)S(1)}, s32[]{:S(2)}) async-start(f32[4,5,1,32,256]{4,0,3,1,2:T(4,128)} %copy-done.2), calls=%async_computation.1 | async-start | bytes 81920 | tf_op jit(solution)/shard_map/slice | solution.py:72
